TPU v7x, 32 devices: a whole 2x2x4 slice. The times are simulated.
32 devices in a mesh: dp: 8 (over z, x), tensor: 4 (over y, core).
Axes of the slice: x: 2, y: 2, z: 4, core: 2. Of those that a mesh axis runs over, the one named last changes fastest.
Arguments:
- prompt_in: bfloat16 [8192, 1024], P('dp'), may hold values from -6 to 6
- cont_in: bfloat16 [2048, 1024], P('dp'), may hold values from -6 to 6
- prompt_cot: bfloat16 [8192, 1024], P('dp'), may hold values from -6 to 6
- cont_cot: bfloat16 [2048, 1024], P('dp'), may hold values from -6 to 6
- group_of: int32 [16], replicated, may hold values from 0 to 7, as said below
- offsets: int32 [16], replicated, may hold values from 512 to 1024, as said below
- ln1_gain: bfloat16 [1024], replicated, may hold values from 0.5 to 1.5
- ln1_bias: bfloat16 [1024], replicated, may hold values from -4 to 4
- ln2_gain: bfloat16 [1024], replicated, may hold values from 0.5 to 1.5
- ln2_bias: bfloat16 [1024], replicated, may hold values from -4 to 4
- qkv_weight: bfloat16 [1024, 3072], P(None, 'tensor'), may hold values from -0.25 to 0.25
- qkv_bias: bfloat16 [3072], P('tensor'), may hold values from -6 to 6
- dense_weight: bfloat16 [1024, 1024], P('tensor'), may hold values from -2 to 2
- dense_bias: bfloat16 [1024], replicated, may hold values from -4 to 4
- fc1_weight: bfloat16 [1024, 4096], P(None, 'tensor'), may hold values from -0.1875 to 0.1875
- fc1_bias: bfloat16 [4096], P('tensor'), may hold values from -6 to 6
- fc2_weight: bfloat16 [4096, 1024], P('tensor'), may hold values from -0.09375 to 0.09375
- fc2_bias: bfloat16 [1024], replicated, may hold values from -4 to 4
Outputs:
- prompt_out: bfloat16 [8192, 1024], P('dp')
- cont_out: bfloat16 [2048, 1024], P('dp')
- prompt_grad: bfloat16 [8192, 1024], P('dp')
- cont_grad: bfloat16 [2048, 1024], P('dp')
- ln1_gain_grad: float32 [1024], replicated
- ln1_bias_grad: float32 [1024], replicated
- ln2_gain_grad: float32 [1024], replicated
- ln2_bias_grad: float32 [1024], replicated
- qkv_weight_grad: float32 [1024, 3072], P(None, 'tensor')
- qkv_bias_grad: float32 [3072], P('tensor')
- dense_weight_grad: float32 [1024, 1024], P('tensor')
- dense_bias_grad: float32 [1024], replicated
- fc1_weight_grad: float32 [1024, 4096], P(None, 'tensor')
- fc1_bias_grad: float32 [4096], P('tensor')
- fc2_weight_grad: float32 [4096, 1024], P('tensor')
- fc2_bias_grad: float32 [1024], replicated
Inputs may be any that keep to these rules, and one draw needn't show every extreme that they name: `group_of`: each of the 8 groups is named by exactly 2 continuations. Continuation j sees the first offsets[j] tokens of its group's prompt, and its tokens stand at positions offsets[j] onward.
All inputs are finite; a program needn't handle non-finite values.
Results may differ from a plain program's by a relative error of at most 0.017.
The roundings to bfloat16 on the way count: a program that leaves them out, or rounds other values in their place, can miss the bound.
Values may be sent and summed in bfloat16 or wider, within the bound.
A program may use at most 256 MiB of HBM per device.

v0:
```python
import functools
import math

import jax
import jax.numpy as jnp
import numpy as np
from jax import lax
from jax.experimental import pallas as pl
from jax.experimental.pallas import tpu as pltpu
from jax.sharding import PartitionSpec as P

HD = 64
ROT = 16
CONT_LEN = 128
TILE = 256
CHUNK = 128
MEMBERS = 2

eps_norm = 1e-05
masked_value = -1e30
MESH = pl.DeviceIdType.MESH
bf16 = jnp.bfloat16
f32 = jnp.float32


def dot(a, b):
    return jnp.dot(a, b, preferred_element_type=f32)


def dot_nt(a, b):
    return lax.dot_general(a, b, (((1,), (1,)), ((), ())), preferred_element_type=f32)


def dot_tn(a, b):
    return lax.dot_general(a, b, (((0,), (0,)), ((), ())), preferred_element_type=f32)


def row_stats(x):
    centered = x - jnp.mean(x, axis=-1, keepdims=True)
    scale = lax.rsqrt(jnp.mean(centered * centered, axis=-1, keepdims=True) + eps_norm)
    return centered * scale, scale


def norm_pull(x, e):
    xhat, scale = row_stats(x)
    return scale * (
        e
        - jnp.mean(e, axis=-1, keepdims=True)
        - xhat * jnp.mean(e * xhat, axis=-1, keepdims=True)
    )


def gelu_and_slope(u):
    t = 1.0 / (1.0 + jnp.abs(u) * (0.3275911 / math.sqrt(2.0)))
    bell = jnp.exp(-0.5 * u * u)
    poly = t * (
        0.127414796
        + t * (-0.142248368 + t * (0.7107068705 + t * (-0.7265760135 + t * 0.5307027145)))
    )
    tail = poly * bell
    cdf = jnp.where(u >= 0, 1.0 - tail, tail)
    return u * cdf, cdf + u * bell * (1.0 / math.sqrt(2.0 * math.pi))


def rotary_table(length):
    half = ROT // 2
    frequencies = np.exp(
        -np.arange(half, dtype=np.float32) * np.float32(2.0 * math.log(10000.0) / ROT)
    ).astype(np.float32)
    angles = np.arange(length, dtype=np.float32)[:, None] * frequencies[None, :]
    angles = np.concatenate([angles, angles], axis=1).astype(np.float32)
    cos = np.ones((length, HD), np.float32)
    low = np.zeros((length, HD), np.float32)
    high = np.zeros((length, HD), np.float32)
    cos[:, :ROT] = np.cos(angles)
    low[:, :half] = -np.sin(angles)[:, :half]
    high[:, half:ROT] = np.sin(angles)[:, half:]
    return np.stack([np.concatenate([t, t], axis=1) for t in (cos, low, high)])


def ring_spot(device, n):
    odd = lax.rem(device, jnp.int32(2))
    half = lax.div(device, jnp.int32(2))
    return (1 - odd) * half + odd * (n - 1 - half)


def ring_device(spot, n):
    far = lax.div(spot, jnp.int32(n // 2))
    return (1 - far) * (2 * spot) + far * (2 * (n - 1 - spot) + 1)


def ring_neighbours(n):
    spot = ring_spot(lax.axis_index("dp"), n)
    after = ring_device(lax.rem(spot + 1, jnp.int32(n)), n)
    before = ring_device(lax.rem(spot + n - 1, jnp.int32(n)), n)
    return spot, after, before


def find_members(group_ref, wanted):
    count = group_ref.shape[0]
    first = jnp.int32(count)
    last = jnp.int32(-1)
    for j in range(count):
        hit = group_ref[j] == wanted
        first = jnp.minimum(first, jnp.where(hit, jnp.int32(j), jnp.int32(count)))
        last = jnp.maximum(last, jnp.where(hit, jnp.int32(j), jnp.int32(-1)))
    return jnp.minimum(first, count - 1), jnp.maximum(last, 0)


def remote(src, dst, send, recv, device):
    return pltpu.make_async_remote_copy(
        src_ref=src, dst_ref=dst, send_sem=send, recv_sem=recv, device_id=device, device_id_type=MESH
    )


def as_row(ref):
    return ref[...].astype(f32).reshape(1, ref.shape[0])


def span(start, size, step):
    return pl.ds(pl.multiple_of(start, step), size)


def piece_rows(rows, n):
    return rows // (2 * n), max(16, rows // (2 * n))


def ring_shape(rows, width, n):
    return (n, 2, piece_rows(rows, n)[1], width)


def put_tile(buffer, k, value, rows, n, cols=slice(None)):
    size = piece_rows(rows, n)[0]
    pieces = TILE // size
    for p in range(pieces):
        buffer[k * (pieces // 2) + p // 2, p % 2, :size, cols] = value[p * size : (p + 1) * size].astype(bf16)


def pair_columns(c0, c1, c2, lane):
    low = lane < HD
    crossed = jnp.where(low, c2, c0)
    return jnp.where(low, c0, c1), pltpu.roll(crossed, HD, 1), jnp.where(low, c1, c2)


def unpair_columns(q, k, v, lane):
    low = lane < HD
    crossed = pltpu.roll(k, HD, 1)
    return jnp.where(low, q, crossed), jnp.where(low, v, q), jnp.where(low, crossed, v)


class RingSum:
    def __init__(self, buffer, arrived, send, recv, n):
        self.buffer, self.arrived, self.send, self.recv, self.n = buffer, arrived, send, recv, n
        self.spot, self.after, self.before = ring_neighbours(n)

    def copies(self, k):
        n = self.n
        ahead = lax.rem(self.spot + (2 * n - 1) - k, jnp.int32(n))
        back = lax.rem(self.spot + 1 + k, jnp.int32(n))
        return [
            remote(
                self.buffer.at[chunk, way], self.arrived.at[k, way], self.send.at[way, k], self.recv.at[way, k],
                {"dp": device},
            )
            for way, (chunk, device) in enumerate(((ahead, self.after), (back, self.before)))
        ]

    def start(self, k):
        for c in self.copies(k):
            c.start()

    def finish(self, k):
        n = self.n
        for c in self.copies(k):
            c.wait()
        for way, chunk in enumerate(
            (lax.rem(self.spot + (2 * n - 2) - k, jnp.int32(n)), lax.rem(self.spot + 2 + k, jnp.int32(n)))
        ):
            self.buffer[chunk, way] += self.arrived[k, way]


class RingGather:
    def __init__(self, buffer, send, recv, n, part=()):
        self.buffer, self.send, self.recv, self.n, self.part = buffer, send, recv, n, part
        self.spot, self.after, self.before = ring_neighbours(n)

    def copies(self, k):
        n = self.n
        ahead = lax.rem(self.spot + n - k, jnp.int32(n))
        back = lax.rem(self.spot + k, jnp.int32(n))
        return [
            remote(
                self.buffer.at[(chunk, way) + self.part], self.buffer.at[(chunk, way) + self.part],
                self.send.at[way, k], self.recv.at[way, k], {"dp": device},
            )
            for way, (chunk, device) in enumerate(((ahead, self.after), (back, self.before)))
        ]

    def start(self, k):
        for c in self.copies(k):
            c.start()

    def finish(self, k):
        for c in self.copies(k):
            c.wait()


def advance(summing, gathering, t, stop):
    n = summing.n

    @pl.when(t < n - 1)
    def _():
        summing.finish(t)

    @pl.when(t < n - 2)
    def _():
        summing.start(t + 1)

    @pl.when((t == n - 2) & (stop > n - 1))
    def _():
        gathering.start(jnp.int32(0))

    @pl.when((t >= n - 1) & (t < stop))
    def _():
        gathering.finish(t - (n - 1))

    @pl.when((t >= n - 1) & (t < stop - 1))
    def _():
        gathering.start(t - (n - 2))


def layer_kernel(
    n_dp, n_tensor, early, group_ref, offsets, xp, xc, dp, dc, w1, w2, wqkv, wd, table,
    gain_two_ref, shift_two_ref, bias1_ref, gain_one_ref, shift_one_ref, bias_qkv_ref, bias_one_ref, bias_two_ref,
    out_p, out_c, grad_p, grad_c, w1s_out, w2s_out, wg_out, stack, vec_out,
    x_all, dy_all, w1_v, w2_v, wqkv_v, wd_v, tab, h_all, g_all, mixed, da_all, ring, moved,
    sum1, sum2, got1, got2, wg, qs, dos, ks, vs, k_turned, v_turned, dks, dvs, o_all, y_home,
    rc, ry, own_rows, keep_y, keep_d, fin, small, small_core, small_y, small_ring,
    own_sem, load_sem, out_sem, part_sem, home_sem, ring_send, ring_recv, y_send, y_recv, core_send, core_recv,
    rs_send, rs_recv, ag_send, ag_recv,
    fill_sem, rc_send, rc_recv, ry_send, ry_recv, gl_send, gl_recv, gc_send, gc_recv,
    home_send, home_recv, sc_send, sc_recv, sy_send, sy_recv, fin_send, fin_recv, finc_send, finc_recv,
    rows_sem, outc_sem, x_send, x_recv, xg_send, xg_recv,
):
    prompt_len, width = xp.shape
    cont_total = xc.shape[0]
    conts = MEMBERS
    rows = prompt_len + cont_total
    tiles = rows // TILE
    prompt_tiles = prompt_len // TILE
    hidden = w1.shape[1]
    local = wd.shape[0]
    heads = local // HD
    piece = CONT_LEN // n_tensor
    lines = n_tensor // 2
    table_len = table.shape[1]
    scale = 1.0 / math.sqrt(HD)
    me_dp, me_t = lax.axis_index("dp"), lax.axis_index("tensor")
    core = lax.rem(me_t, jnp.int32(2))
    sibling = me_t + 1 - 2 * core
    peers = [lax.rem(me_t + 2 * k, jnp.int32(n_tensor)) for k in range(1, lines)]
    spot, after, before = ring_neighbours(n_dp)

    own = [
        pltpu.make_async_copy(
            src.at[span(s * CONT_LEN + me_t * piece, piece, 16)], ring.at[spot, a, s], own_sem.at[a, s]
        )
        for a, src in enumerate((xc, dc))
        for s in range(conts)
    ]
    loads = [
        pltpu.make_async_copy(src, dst, load_sem.at[i])
        for i, (src, dst) in enumerate(
            (
                (xc, x_all.at[pl.ds(0, cont_total)]),
                (w1, w1_v),
                (dc, dy_all.at[pl.ds(0, cont_total)]),
                (w2, w2_v),
                (xp, x_all.at[pl.ds(cont_total, prompt_len)]),
                (dp, dy_all.at[pl.ds(cont_total, prompt_len)]),
                (wqkv, wqkv_v),
                (wd, wd_v),
                (table, tab.at[:, pl.ds(0, table_len)]),
            )
        )
    ]
    partners = [{"dp": after}, {"dp": before}, {"tensor": sibling}] + [{"tensor": p} for p in peers]
    barrier = pltpu.get_barrier_semaphore()
    for partner in partners:
        pl.semaphore_signal(barrier, inc=1, device_id=partner, device_id_type=MESH)
    for c in own + [loads[i] for i in (1, 0, 4, 2, 5, 3, 6, 7, 8)]:
        c.start()
    pl.semaphore_wait(barrier, len(partners))

    halves = min(2, piece // 16)
    moving = [
        RingGather(
            ring, ring_send.at[s, b], ring_recv.at[s, b], n_dp, (s, pl.ds(b * (piece // halves), piece // halves))
        )
        for s in range(conts)
        for b in range(halves)
    ]
    for s in range(conts):
        for b in range(halves):
            for way, (src, device) in enumerate(((xc, after), (dc, before))):
                at = span(s * CONT_LEN + me_t * piece + b * (piece // halves), piece // halves, 16)
                part = pl.ds(b * (piece // halves), piece // halves)
                remote(
                    src.at[at], ring.at[spot, way, s, part], ring_send.at[s, b, way, 0], ring_recv.at[s, b, way, 0],
                    {"dp": device},
                ).start()
    sums = [
        (
            RingSum(buffer, got, rs_send.at[i], rs_recv.at[i], n_dp),
            RingGather(buffer, ag_send.at[i], ag_recv.at[i], n_dp),
        )
        for i, (buffer, got) in enumerate(((sum2, got2), (sum1, got1)))
    ]

    def spread(point, points, total, step):
        begin = lax.div(point * total, jnp.int32(points))
        end = lax.div((point + 1) * total, jnp.int32(points))

        def one(t, _):
            step(t)
            return 0

        lax.fori_loop(begin, end, one, 0)

    def move_step(t):
        k = lax.div(t, jnp.int32(len(moving)))
        for s, m in enumerate(moving):
            mine = lax.rem(t, jnp.int32(len(moving))) == s

            @pl.when(mine)
            def _():
                m.finish(k)

            @pl.when(mine & (k < n_dp - 2))
            def _():
                m.start(k + 1)

    move_points = 2 * tiles + hidden // TILE

    def move(point):
        spread(point, move_points, len(moving) * (n_dp - 1), move_step)

    stop = 2 * (n_dp - 1)
    lead = 3
    all_turns = 2 * (n_dp - 1 + early) - 1
    pair_turns = all_turns * 2 // (3 * heads // 2)
    project_turns = all_turns // 9
    back_turns = (all_turns - project_turns - pair_turns * (heads // 2)) // 2
    back_from = project_turns + pair_turns * (heads // 2)
    block_ends = (8, 14, 19, 22, 32, 35)

    def sum_step(t):
        k = lax.div(t, jnp.int32(2))

        @pl.when(lax.rem(t, jnp.int32(2)) == 0)
        def _():
            advance(*sums[1], k, stop)

        @pl.when((lax.rem(t, jnp.int32(2)) == 1) & (k + lead < stop))
        def _():
            advance(*sums[0], k + lead, stop)

    def turn(begin, end):
        def one(t, _):
            sum_step(t)
            return 0

        lax.fori_loop(begin, end, one, 0)

    def turn_evenly(base, point, points, total):
        spread(point, points, total, lambda t: sum_step(base + t))

    def turn_block(pair, place):
        base = project_turns + pair * pair_turns
        ends = [pair_turns * b // block_ends[-1] for b in (0,) + block_ends]
        if ends[place] < ends[place + 1]:
            turn(base + ends[place], base + ends[place + 1])

    few = conts * piece
    quarter = prompt_len // n_tensor

    def deal(src, prompt_row, cont_row, prompt_base, cont_base, which):
        copies = []
        for q in range(n_tensor):
            copies.append(
                pltpu.make_async_copy(
                    src.at[pl.ds(prompt_row + q * quarter, quarter)], stack.at[q, pl.ds(prompt_base, quarter)],
                    part_sem.at[which, q, conts],
                )
            )
            for s in range(conts):
                copies.append(
                    pltpu.make_async_copy(
                        src.at[pl.ds(cont_row + s * CONT_LEN + q * piece, piece)],
                        stack.at[q, pl.ds(cont_base + s * piece, piece)], part_sem.at[which, q, s],
                    )
                )
        return copies

    deal_da2 = deal(da_all, cont_total, 0, 4 * few + quarter, 3 * few, 0)
    deal_da1 = deal(da_all, 0, prompt_len, 4 * few, 2 * few, 1)
    deal_y = deal(da_all, 0, prompt_len, 4 * few + 2 * quarter, 0, 2)
    deal_home = [
        pltpu.make_async_copy(
            y_home.at[pl.ds(s * CONT_LEN + q * piece, piece)], stack.at[q, pl.ds(few + s * piece, piece)],
            home_sem.at[q, s],
        )
        for q in range(n_tensor)
        for s in range(conts)
    ]
    outs = [
        pltpu.make_async_copy(src, dst, out_sem.at[i])
        for i, (src, dst) in enumerate(((sum1, w1s_out), (sum2, w2s_out), (wg, wg_out)))
    ]
    small[...] = jnp.zeros_like(small)

    gain, shift, bias = as_row(gain_two_ref), as_row(shift_two_ref), as_row(bias1_ref)
    loads[0].wait()
    loads[1].wait()

    def mlp_forward(i, _):
        @pl.when(i == 1)
        def _():
            loads[4].wait()

        at = span(i * TILE, TILE, TILE)
        xhat, _ = row_stats(x_all[at].astype(f32))
        h = (xhat * gain + shift).astype(bf16)
        h_all[at] = h
        for k in range(hidden // TILE):
            cols = slice(k * TILE, (k + 1) * TILE)
            value, slope = gelu_and_slope(dot(h, w1_v[:, cols]) + bias[:, cols])
            g_all[at, cols] = value.astype(bf16)
            mixed[at, cols] = slope.astype(bf16)
        move(i)
        return 0

    lax.fori_loop(0, tiles, mlp_forward, 0)
    loads[2].wait()
    loads[5].wait()

    def down_tile(k, _):
        cols = span(k * TILE, TILE, TILE)
        put_tile(sum2, k, dot_tn(g_all[:, cols], dy_all[:rows]), hidden, n_dp)
        move(tiles + k)
        return 0

    lax.fori_loop(0, hidden // TILE, down_tile, 0)
    sums[0][0].start(jnp.int32(0))
    members = find_members(group_ref, me_dp)
    offs = [offsets[m] for m in members]
    for c in loads[6:]:
        c.wait()
    for m, off in enumerate(offs):
        for a in range(3):
            tab[a, table_len + m * CONT_LEN : table_len + (m + 1) * CONT_LEN, :] = tab[a, pl.ds(off, CONT_LEN), :]
    lane = lax.broadcasted_iota(jnp.int32, (1, CHUNK), 1)
    bias_qkv = as_row(bias_qkv_ref)
    biases = []
    for pair in range(heads // 2):
        chunks = [slice((3 * pair + c) * CHUNK, (3 * pair + c + 1) * CHUNK) for c in range(3)]
        biases += pair_columns(*(bias_qkv[:, cols] for cols in chunks), lane)
        for cols, value in zip(chunks, pair_columns(*(wqkv_v[:, cols] for cols in chunks), lane)):
            wqkv_v[:, cols] = value

    loads[3].wait()

    def mlp_backward(i, _):
        at = span(i * TILE, TILE, TILE)
        dy = dy_all[at]
        for k in range(hidden // TILE):
            cols = slice(k * TILE, (k + 1) * TILE)
            du = (dot_nt(dy, w2_v[cols, :]) * mixed[at, cols].astype(f32)).astype(bf16)
            mixed[at, cols] = du
            small[5:6, cols] += jnp.sum(du.astype(f32), axis=0, keepdims=True)
        da = dot_nt(mixed[at, :hidden], w1_v[...])
        da_all[at] = da.astype(bf16)
        xhat, _ = row_stats(x_all[at].astype(f32))
        small[2:3] += jnp.sum(da * xhat, axis=0, keepdims=True)
        small[3:4] += jnp.sum(da, axis=0, keepdims=True)
        small[4:5] += jnp.sum(dy.astype(f32), axis=0, keepdims=True)
        move(tiles + hidden // TILE + i)

        @pl.when((lax.rem(i, jnp.int32(2)) == 0) & (i > 0) & (lax.div(i, jnp.int32(2)) < lead))
        def _():
            advance(*sums[0], lax.div(i, jnp.int32(2)) - 1, stop)

        return 0

    lax.fori_loop(0, tiles, mlp_backward, 0)
    for c in deal_da2:
        c.start()

    for c in own:
        c.wait()
    for m, member in enumerate(members):
        where = ring_spot(lax.div(member, jnp.int32(conts)), n_dp)
        slot = lax.rem(member, jnp.int32(conts))
        for a in range(2):
            moved[me_t, a, m] = ring[where, a, slot]
    over_y = [
        remote(moved.at[me_t], moved.at[me_t], y_send.at[k], y_recv.at[k], {"tensor": p})
        for k, p in enumerate(peers)
    ]
    over_core = [
        remote(
            moved.at[2 * j + core], moved.at[2 * j + core], core_send.at[j], core_recv.at[j], {"tensor": sibling}
        )
        for j in range(lines)
    ]
    for c in over_y:
        c.start()

    def up_tile(k, _):
        cols = span(k * TILE, TILE, TILE)
        put_tile(sum1, k, dot_tn(h_all[:, cols], mixed[:, :hidden]), width, n_dp)
        return 0

    lax.fori_loop(0, width // TILE, up_tile, 0)
    sums[1][0].start(jnp.int32(0))
    advance(*sums[0], jnp.int32(lead - 1), stop)

    gain, shift = as_row(gain_one_ref), as_row(shift_one_ref)

    def turned(z, start, sign):
        cos, low, high = (tab[a, pl.ds(start, TILE), :] for a in range(3))
        half = ROT // 2
        return z * cos + (pltpu.roll(z, CHUNK - half, 1) * low + pltpu.roll(z, half, 1) * high) * sign

    def table_start(i):
        return pl.multiple_of(i * TILE + lax.div(i, jnp.int32(prompt_tiles)) * (table_len - prompt_len), CHUNK)

    def project(i):
        at = span(i * TILE, TILE, TILE)
        source = span(i * TILE + cont_total, TILE, TILE)
        xhat, _ = row_stats(x_all[source].astype(f32))
        h = (xhat * gain + shift).astype(bf16)
        h_all[at] = h
        do = dot_nt(dy_all[source], wd_v[...]).astype(bf16)
        for pair in range(heads // 2):
            q, k, v = (
                dot(h, wqkv_v[:, c * CHUNK : (c + 1) * CHUNK]) + biases[c] for c in range(3 * pair, 3 * pair + 3)
            )
            q = turned(q, table_start(i), 1.0)
            qs[2 * pair, at] = jnp.where(lane < HD, q, 0.0).astype(bf16)
            qs[2 * pair + 1, at] = jnp.where(lane < HD, 0.0, q).astype(bf16)
            k = turned(k, table_start(i), 1.0)
            ks[pair, at] = k.astype(bf16)
            k_turned[pair, :, at] = k.T.astype(bf16)
            vs[pair, at] = v.astype(bf16)
            v_turned[pair, :, at] = v.T.astype(bf16)
            both = do[:, pair * CHUNK : (pair + 1) * CHUNK].astype(f32)
            dos[2 * pair, at] = jnp.where(lane < HD, both, 0.0).astype(bf16)
            dos[2 * pair + 1, at] = jnp.where(lane < HD, 0.0, both).astype(bf16)

    def project_prompt(i, _):
        project(i)
        turn_evenly(0, i, prompt_tiles, project_turns)
        return 0

    lax.fori_loop(0, prompt_tiles, project_prompt, 0)
    for c in over_y:
        c.wait()
    for c in over_core:
        c.start()

    query_lane = lax.broadcasted_iota(jnp.int32, (1, TILE), 1)
    reach = jnp.zeros((1, TILE), jnp.int32)
    for m, off in enumerate(offs):
        reach = jnp.where(lax.div(query_lane, jnp.int32(CONT_LEN)) == m, off, reach)

    def attend(pair, _):
        for block in list(range(prompt_tiles - 1, -1, -1)) + [prompt_tiles]:
            first = block * TILE
            seen = first + TILE
            at = slice(first, seen)
            if block == prompt_tiles:
                @pl.when(pair == 0)
                def _():
                    for c in over_core:
                        c.wait()
                    for q in range(n_tensor):
                        for s in range(conts):
                            to = rows + s * CONT_LEN + q * piece
                            x_all[to : to + piece, :] = moved[q, 0, s]
                            dy_all[to : to + piece, :] = moved[q, 1, s]
                    project(jnp.int32(prompt_tiles))

            k, v = ks[pair, :seen], vs[pair, :seen]
            key = lax.broadcasted_iota(jnp.int32, (TILE, TILE), 0)
            query = lax.broadcasted_iota(jnp.int32, (TILE, TILE), 1)
            seen_near = key <= query
            if block == prompt_tiles:
                key_row = lax.broadcasted_iota(jnp.int32, (prompt_len, TILE), 0)
                same = lax.div(key, jnp.int32(CONT_LEN)) == lax.div(query, jnp.int32(CONT_LEN))
                seen_near = seen_near & same
            heads_now = (2 * pair, 2 * pair + 1)
            scores = [dot_nt(k, qs[h, at]) * scale for h in heads_now]
            dprobs = [dot_nt(v, dos[h, at]) for h in heads_now]
            lows, low_slopes, o_turned, dq_turned = [], [], [], []
            for sub in range(2):
                s, dprob = scores[sub], dprobs[sub]
                near = jnp.where(seen_near, s[first:], masked_value)
                if block == prompt_tiles:
                    s = jnp.concatenate([jnp.where(key_row < reach, s[:first], masked_value), near], axis=0)
                else:
                    s = near if first == 0 else jnp.concatenate([s[:first], near], axis=0)
                p = jnp.exp(s - jnp.max(s, axis=0, keepdims=True))
                p = p * (1.0 / jnp.sum(p, axis=0, keepdims=True))
                low = p.astype(bf16)
                delta = jnp.sum(p * dprob, axis=0, keepdims=True)
                ds = (p * (dprob - delta)).astype(bf16)
                part = slice(sub * HD, (sub + 1) * HD)
                o_turned.append(dot(v_turned[pair, part, :seen], low))
                dq_turned.append(dot(k_turned[pair, part, :seen], ds))
                lows.append(low)
                low_slopes.append(ds)
            o_all[at, span(pair * CHUNK, CHUNK, CHUNK)] = jnp.concatenate(o_turned, axis=0).T.astype(bf16)
            dq = jnp.concatenate(dq_turned, axis=0).T * scale
            dq = turned(dq, table_start(jnp.int32(block)), -1.0).astype(bf16)
            cols = span(3 * pair * CHUNK, CHUNK, CHUNK)
            mixed[at, cols] = dq
            small[6:7, cols] += jnp.sum(dq.astype(f32), axis=0, keepdims=True)
            q_both = jnp.concatenate([qs[h, at] for h in heads_now], axis=0)
            do_both = jnp.concatenate([dos[h, at] for h in heads_now], axis=0)
            dk = dot(jnp.concatenate(low_slopes, axis=1), q_both)
            dv = dot(jnp.concatenate(lows, axis=1), do_both)
            if block == prompt_tiles - 1:
                dks[:seen] = dk
                dvs[:seen] = dv
            else:
                old = min(seen, prompt_len)
                dks[:old] += dk[:old]
                dvs[:old] += dv[:old]
                if old < seen:
                    dks[old:seen] = dk[old:]
                    dvs[old:seen] = dv[old:]
            turn_block(pair, prompt_tiles - 1 - block if block < prompt_tiles else block)

        for i in range(tiles):
            at = slice(i * TILE, (i + 1) * TILE)
            dk = turned(dks[at] * scale, table_start(jnp.int32(i)), -1.0).astype(bf16)
            for c, value in ((1, dk), (2, dvs[at].astype(bf16))):
                cols = span((3 * pair + c) * CHUNK, CHUNK, CHUNK)
                mixed[at, cols] = value
                small[6:7, cols] += jnp.sum(value.astype(f32), axis=0, keepdims=True)
        turn_block(pair, 5)
        return 0

    lax.fori_loop(0, heads // 2, attend, 0)
    for c in deal_da2:
        c.wait()

    def weight_tile(k, _):
        cols = span(k * TILE, TILE, TILE)
        put_tile(wg, k, dot_tn(h_all[:, cols], mixed[:, : 3 * local]), width, n_dp, slice(0, 3 * local))
        put_tile(wg, k, dot_tn(dy_all[cont_total:, cols], o_all[...]), width, n_dp, slice(3 * local, 4 * local))
        turn_evenly(back_from, k, width // TILE, all_turns - back_from - back_turns)
        return 0

    lax.fori_loop(0, width // TILE, weight_tile, 0)
    summing = RingSum(wg, got1, x_send, x_recv, n_dp)
    gathering = RingGather(wg, xg_send, xg_recv, n_dp)
    cont_from = 4
    rest_ticks = 2 * stop - all_turns
    all_ticks = max(stop, rest_ticks, cont_from + n_dp - 1)
    summing.start(jnp.int32(0))

    def back(i, _):
        at = span(i * TILE, TILE, TILE)
        da = dot_nt(mixed[at, : 3 * local], wqkv_v[...])
        da_all[at] = da.astype(bf16)
        xhat, _ = row_stats(x_all[span(i * TILE + cont_total, TILE, TILE)].astype(f32))
        small[0:1] += jnp.sum(da * xhat, axis=0, keepdims=True)
        small[1:2] += jnp.sum(da, axis=0, keepdims=True)

        turn_evenly(all_turns - back_turns, i, tiles, back_turns)
        return 0

    lax.fori_loop(0, tiles, back, 0)
    for c in deal_da1:
        c.start()

    def home_steps(k):
        ahead = lax.rem(spot - k + n_dp, jnp.int32(n_dp))
        back = lax.rem(spot + k, jnp.int32(n_dp))
        return (
            remote(ring.at[ahead, 0], ring.at[ahead, 0], home_send.at[0, k], home_recv.at[0, k], {"dp": after}),
            remote(ring.at[back, 1], ring.at[back, 1], home_send.at[1, k], home_recv.at[1, k], {"dp": before}),
            remote(
                small_ring.at[ahead, 0], small_ring.at[ahead, 0], home_send.at[2, k], home_recv.at[2, k], {"dp": after}
            ),
            remote(
                small_ring.at[back, 1], small_ring.at[back, 1], home_send.at[3, k], home_recv.at[3, k], {"dp": before}
            ),
        )

    def run_ticks(begin, end):
        def one(t, _):
            advance(summing, gathering, t, 2 * (n_dp - 1))

            @pl.when(t < rest_ticks)
            def _():
                sum_step(all_turns + t)

            k = t - cont_from

            @pl.when((k >= 0) & (k < n_dp - 1))
            def _():
                for c in home_steps(k):
                    c.wait()

            @pl.when((k >= 0) & (k < n_dp - 2))
            def _():
                for c in home_steps(k + 1):
                    c.start()

            return 0

        lax.fori_loop(begin, end, one, 0)

    line = lax.div(me_t, jnp.int32(2))
    base_one, base_two, base_y = 4 * few, 4 * few + quarter, 4 * few + 2 * quarter
    depth = base_y + quarter
    group_rows = ((0, base_one), (base_one, 2 * quarter), (base_y, quarter))
    room = rows // depth

    def own_part(m, start, size):
        return (h_all, da_all)[m // room].at[pl.ds((m % room) * depth + start, size)]

    def fill(n, m):
        j = lax.rem(line + (m + 1), jnp.int32(lines))
        return pltpu.make_async_copy(
            stack.at[2 * j + core, pl.ds(*group_rows[n])], own_part(m, *group_rows[n]), fill_sem.at[n, m]
        )

    def to_core(n):
        at = pl.ds(*group_rows[n])
        return [
            remote(
                stack.at[2 * j + 1 - core, at], rc.at[j, at], rc_send.at[n, j], rc_recv.at[n, j], {"tensor": sibling}
            )
            for j in range(lines)
        ]

    def to_line(n):
        return [
            remote(
                own_part(k, *group_rows[n]), ry.at[k, pl.ds(*group_rows[n])], ry_send.at[n, k], ry_recv.at[n, k],
                {"tensor": p},
            )
            for k, p in enumerate(peers)
        ]

    def pass_on(n):
        for c in to_core(n):
            c.wait()
        for k in range(lines - 1):
            j = lax.rem(line + (k + 1), jnp.int32(lines))
            mine = own_part(k, *group_rows[n])
            mine[...] = (mine[...].astype(f32) + rc[j, pl.ds(*group_rows[n])].astype(f32)).astype(bf16)
        for c in to_line(n):
            c.start()

    small_to_core = remote(small, small_core, sc_send, sc_recv, {"tensor": sibling})
    small_to_core.start()
    for c in deal_da1:
        c.wait()
    for c in to_core(1):
        c.start()

    def y_tile(i, _):
        at = span(i * TILE, TILE, TILE)
        total = dot(o_all[at], wd_v[...]) + dot(g_all[span(i * TILE + cont_total, TILE, TILE)], w2_v[...])
        da_all[at] = total.astype(bf16)
        return 0

    lax.fori_loop(0, prompt_tiles, y_tile, 0)
    da_all[prompt_len:] = dot(o_all[prompt_len:], wd_v[...]).astype(bf16)
    y_home[...] = dot(g_all[:cont_total], w2_v[...]).astype(bf16)
    for c in deal_y + deal_home:
        c.start()
    run_ticks(0, 1)
    for c in deal_y + deal_home:
        c.wait()
    for n in (0, 2):
        for c in to_core(n):
            c.start()
    fills = [fill(n, m) for n in (0, 1, 2) for m in range(lines)]
    for c in fills:
        c.start()
    small_to_core.wait()
    row = lax.broadcasted_iota(jnp.int32, (8, 1), 0)
    small_y[line] = small[...] + jnp.where(row < 4, small_core[...], 0.0)
    small_to_line = [
        remote(small_y.at[line], small_y.at[line], sy_send.at[k], sy_recv.at[k], {"tensor": p})
        for k, p in enumerate(peers)
    ]
    for c in small_to_line:
        c.start()
    for c in fills:
        c.wait()
    pass_on(0)
    run_ticks(1, 2)
    pass_on(1)
    pass_on(2)
    for c in small_to_line:
        c.wait()
    reduced = small_y[0]
    for j in range(1, lines):
        reduced = reduced + small_y[j]
    reduced = jnp.where(row < 4, reduced, small[...]).astype(bf16)
    fold = width // 4
    for part in range(4):
        small_ring[spot, part // 2, part % 2 * 8 : part % 2 * 8 + 8] = reduced[:, part * fold : (part + 1) * fold]
    run_ticks(2, cont_from)

    def summed(start, size):
        total = own_part(lines - 1, start, size)[...].astype(f32) + rc[line, pl.ds(start, size)].astype(f32)
        for k in range(lines - 1):
            total = total + ry[k, pl.ds(start, size)].astype(f32)
        return total

    def quarter_rows(q):
        return pl.ds(pl.multiple_of(q * quarter, 16), quarter)

    gain_two = as_row(gain_two_ref)
    both = as_row(bias_one_ref) + as_row(bias_two_ref)
    results = (out_p, grad_p)

    def gather_line(a):
        at = quarter_rows(me_t)
        return [pltpu.make_async_copy(own_rows.at[a], results[a].at[at], rows_sem.at[a])] + [
            remote(own_rows.at[a], results[a].at[at], gl_send.at[a, k], gl_recv.at[a, k], {"tensor": p})
            for k, p in enumerate(peers)
        ]

    def to_sibling(a):
        at = quarter_rows(me_t)
        return [remote(own_rows.at[a], results[a].at[at], gc_send.at[a, 0], gc_recv.at[a, 0], {"tensor": sibling})]

    def gather_core(a):
        copies = []
        for k in range(1, lines):
            at = quarter_rows(2 * lax.rem(line + k, jnp.int32(lines)) + core)
            copies.append(
                remote(results[a].at[at], results[a].at[at], gc_send.at[a, k], gc_recv.at[a, k], {"tensor": sibling})
            )
        return copies

    for c in to_line(0):
        c.wait()
    for s in range(conts):
        ring[spot, 0, s] = summed(s * piece, piece).astype(bf16)
        theirs = x_all[span(rows + s * CONT_LEN + me_t * piece, piece, 16)].astype(f32)
        ring[spot, 1, s] = norm_pull(theirs, summed(2 * few + s * piece, piece) * gain).astype(bf16)
        home = span(s * CONT_LEN + me_t * piece, piece, 16)
        x_home = x_all[home].astype(f32)
        keep_y[s] = x_home + summed(few + s * piece, piece) + both
        pulled = norm_pull(x_home, summed(3 * few + s * piece, piece) * gain_two)
        keep_d[s] = dy_all[home].astype(f32) + pulled
    for c in home_steps(jnp.int32(0)):
        c.start()
    run_ticks(cont_from, cont_from + 3)
    quarter_at = span(cont_total + me_t * quarter, quarter, 16)
    for c in to_line(1):
        c.wait()
    e = summed(base_one, quarter) * gain + summed(base_two, quarter) * gain_two
    own_rows[1] = (dy_all[quarter_at].astype(f32) + norm_pull(x_all[quarter_at].astype(f32), e)).astype(bf16)
    for c in gather_line(1) + to_sibling(1):
        c.start()
    run_ticks(cont_from + 3, cont_from + 5)
    for c in to_line(2):
        c.wait()
    own_rows[0] = (x_all[quarter_at].astype(f32) + summed(base_y, quarter) + both).astype(bf16)
    for c in gather_line(0) + to_sibling(0):
        c.start()
    moved_home = cont_from + n_dp - 1
    run_ticks(cont_from + 5, moved_home)
    for part in range(4):
        at = slice(part % 2 * 8, part % 2 * 8 + 8)
        total = small_ring[0, part // 2, at].astype(f32)
        for j in range(1, n_dp):
            total = total + small_ring[j, part // 2, at].astype(f32)
        vec_out[:, part * fold : (part + 1) * fold] = total
    for s in range(conts):
        mine = me_dp * conts + s
        group = group_ref[mine]
        first, _ = find_members(group_ref, group)
        slot = jnp.where(first == mine, jnp.int32(0), jnp.int32(1))
        where = ring_spot(group, n_dp)
        fin[me_t, 0, s] = (keep_y[s] + ring[where, 0, slot].astype(f32)).astype(bf16)
        fin[me_t, 1, s] = (keep_d[s] + ring[where, 1, slot].astype(f32)).astype(bf16)
    fin_line = [
        remote(fin.at[me_t], fin.at[me_t], fin_send.at[k], fin_recv.at[k], {"tensor": p})
        for k, p in enumerate(peers)
    ]
    fin_core = [
        remote(
            fin.at[2 * j + core], fin.at[2 * j + core], finc_send.at[j], finc_recv.at[j], {"tensor": sibling}
        )
        for j in range(lines)
    ]
    for c in fin_line:
        c.start()
    for c in gather_line(1):
        c.wait()
    for c in gather_core(1):
        c.start()
    run_ticks(moved_home, moved_home + 2)
    for c in gather_line(0):
        c.wait()
    for c in gather_core(0):
        c.start()
    if rest_ticks <= moved_home + 2:
        for c in outs[:2]:
            c.start()
    run_ticks(moved_home + 2, max(moved_home + 2, all_ticks))
    for c in outs if rest_ticks > moved_home + 2 else outs[2:]:
        c.start()
    for c in fin_line:
        c.wait()
    for c in fin_core:
        c.start()
    for c in gather_core(0) + to_sibling(0) + gather_core(1) + to_sibling(1) + fin_core:
        c.wait()
    last = [
        pltpu.make_async_copy(
            fin.at[q, a, s], dst.at[pl.ds(s * CONT_LEN + q * piece, piece)], outc_sem.at[a, q, s]
        )
        for a, dst in ((0, out_c), (1, grad_c))
        for q in range(n_tensor)
        for s in range(conts)
    ]
    for c in last:
        c.start()
    for c in last + outs:
        c.wait()


def run_layer(n_dp, n_tensor, early, group_of, offsets, xp, xc, dp, dc, w1, w2, wqkv, wd, *vectors):
    prompt_len, width = xp.shape
    cont_total = xc.shape[0]
    rows = prompt_len + cont_total
    hidden = w1.shape[1]
    local = wd.shape[0]
    heads = local // HD
    piece = CONT_LEN // n_tensor
    lines = n_tensor // 2
    table = jnp.asarray(rotary_table(prompt_len + CONT_LEN))
    table_rows = table.shape[1] + MEMBERS * CONT_LEN
    up, down = ring_shape(width, hidden, n_dp), ring_shape(hidden, width, n_dp)
    third = ring_shape(width, 4 * local, n_dp)
    quarter = prompt_len // n_tensor
    depth = 4 * MEMBERS * piece + 3 * quarter
    shape = jax.ShapeDtypeStruct
    hbm = pl.BlockSpec(memory_space=pl.ANY)
    vmem = pl.BlockSpec(memory_space=pltpu.VMEM)
    smem = pl.BlockSpec(memory_space=pltpu.SMEM)
    sem = pltpu.SemaphoreType.DMA
    return pl.pallas_call(
        functools.partial(layer_kernel, n_dp, n_tensor, early),
        out_shape=(
            shape(xp.shape, bf16),
            shape(xc.shape, bf16),
            shape(xp.shape, bf16),
            shape(xc.shape, bf16),
            shape(up, bf16),
            shape(down, bf16),
            shape(third, bf16),
            shape((n_tensor, depth, width), bf16),
            shape((8, width), f32),
        ),
        in_specs=[smem] * 2 + [hbm] * 9 + [vmem] * 8,
        out_specs=(hbm,) * 8 + (vmem,),
        scratch_shapes=[
            pltpu.VMEM((rows + cont_total, width), bf16),
            pltpu.VMEM((rows + cont_total, width), bf16),
            pltpu.VMEM((width, hidden), bf16),
            pltpu.VMEM((hidden, width), bf16),
            pltpu.VMEM((width, 3 * local), bf16),
            pltpu.VMEM((local, width), bf16),
            pltpu.VMEM((3, table_rows, CHUNK), f32),
            pltpu.VMEM((rows, width), bf16),
            pltpu.VMEM((rows, hidden), bf16),
            pltpu.VMEM((rows, max(hidden, 3 * local)), bf16),
            pltpu.VMEM((rows, width), bf16),
            pltpu.VMEM((n_dp, 2, MEMBERS, piece, width), bf16),
            pltpu.VMEM((n_tensor, 2, MEMBERS, piece, width), bf16),
            pltpu.VMEM(up, bf16),
            pltpu.VMEM(down, bf16),
            pltpu.VMEM((n_dp - 1,) + up[1:], bf16),
            pltpu.VMEM((n_dp - 1,) + down[1:], bf16),
            pltpu.VMEM(third, bf16),
        ]
        + [pltpu.VMEM((heads, rows, CHUNK), bf16)] * 2
        + [pltpu.VMEM((heads // 2, rows, CHUNK), bf16)] * 2
        + [pltpu.VMEM((heads // 2, CHUNK, rows), bf16)] * 2
        + [pltpu.VMEM((rows, CHUNK), f32)] * 2
        + [
            pltpu.VMEM((rows, local), bf16),
            pltpu.VMEM((cont_total, width), bf16),
            pltpu.VMEM((lines, depth, width), bf16),
            pltpu.VMEM((lines - 1, depth, width), bf16),
            pltpu.VMEM((2, quarter, width), bf16),
            pltpu.VMEM((MEMBERS, piece, width), f32),
            pltpu.VMEM((MEMBERS, piece, width), f32),
            pltpu.VMEM((n_tensor, 2, MEMBERS, piece, width), bf16),
            pltpu.VMEM((8, width), f32),
            pltpu.VMEM((8, width), f32),
            pltpu.VMEM((lines, 8, width), f32),
            pltpu.VMEM((n_dp, 2, 16, width // 4), bf16),
            sem((2, MEMBERS)),
            sem((9,)),
            sem((3,)),
            sem((3, n_tensor, MEMBERS + 1)),
            sem((n_tensor, MEMBERS)),
            sem((MEMBERS, 2, 2, n_dp - 1)),
            sem((MEMBERS, 2, 2, n_dp - 1)),
            sem((lines - 1,)),
            sem((lines - 1,)),
            sem((lines,)),
            sem((lines,)),
        ]
        + [sem((2, 2, n_dp - 1))] * 4
        + [sem((3, lines))] * 3
        + [sem((3, lines - 1))] * 2
        + [sem((2, lines - 1))] * 2
        + [sem((2, lines))] * 2
        + [sem((4, n_dp - 1))] * 2
        + [sem] * 2
        + [sem((lines - 1,))] * 4
        + [sem((lines,))] * 2
        + [sem((2,)), sem((2, n_tensor, MEMBERS))]
        + [sem((2, n_dp - 1))] * 4,
        compiler_params=pltpu.CompilerParams(
            collective_id=0, has_side_effects=True, vmem_limit_bytes=63 * 2**20
        ),
        cost_estimate=pl.CostEstimate(flops=34 * 10**9, bytes_accessed=40 * 10**6, transcendentals=5 * 10**6),
        name="layer",
    )(group_of, offsets, xp, xc, dp, dc, w1, w2, wqkv, wd, table, *vectors)


def finish_kernel(
    groups, out_p, out_c, grad_p, grad_c, w1s, w2s, wg, total,
    out_p_out, out_c_out, grad_p_out, grad_c_out, gain_one, shift_one, gain_two, shift_two,
    qkv_out, qkv_bias, dense_out, dense_bias, w1_out, w1_bias, w2_out, w2_bias,
    out_p_v, out_c_v, grad_p_v, grad_c_v, w1s_v, w2s_v, wg_v, qkv_v, dense_v, w1_v, w2_v,
    copy_in, copy_out, piece_in, piece_out, dense_sem,
):
    local3 = qkv_out.shape[1]
    plain = (
        (out_p, out_p_v, out_p_out), (grad_p, grad_p_v, grad_p_out),
        (out_c, out_c_v, out_c_out), (grad_c, grad_c_v, grad_c_out),
    )
    plain_in = [pltpu.make_async_copy(a, b, copy_in.at[i]) for i, (a, b, _) in enumerate(plain)]
    plain_out = [pltpu.make_async_copy(b, c, copy_out.at[i]) for i, (_, b, c) in enumerate(plain)]
    weights = ((w1s, w1s_v, w1_v, w1_out), (w2s, w2s_v, w2_v, w2_out), (wg, wg_v, qkv_v, qkv_out))

    def chunks_of(a, g):
        return pl.ds(g * (a.shape[0] // groups), a.shape[0] // groups)

    def rows_of(a, g):
        return pl.ds(g * (a.shape[0] // groups), a.shape[0] // groups)

    loads = [
        [pltpu.make_async_copy(a.at[chunks_of(a, g)], b.at[chunks_of(a, g)], piece_in.at[i, g]) for g in range(groups)]
        for i, (a, b, _, _) in enumerate(weights)
    ]
    stores = [
        [pltpu.make_async_copy(c.at[rows_of(c, g)], d.at[rows_of(c, g)], piece_out.at[i, g]) for g in range(groups)]
        for i, (_, _, c, d) in enumerate(weights)
    ]
    for c in plain_in[:1] + loads[0] + plain_in[1:2] + loads[1] + plain_in[2:] + loads[2]:
        c.start()
    lane = lax.broadcasted_iota(jnp.int32, (1, CHUNK), 1)
    pairs = [
        [slice((3 * pair + c) * CHUNK, (3 * pair + c + 1) * CHUNK) for c in range(3)]
        for pair in range(local3 // (3 * CHUNK))
    ]
    for n, dst in enumerate((gain_one, shift_one, gain_two, shift_two, dense_bias, w1_bias)):
        dst[...] = total[n, : dst.shape[0]]
    w2_bias[...] = total[4, :]
    for columns in pairs:
        for cols, value in zip(columns, unpair_columns(*(total[6:7, cols] for cols in columns), lane)):
            qkv_bias[cols] = value[0]

    def pieces(src, dst, g):
        per_group = src.shape[0] // groups
        size = dst.shape[0] // (2 * src.shape[0])
        for p in range(2 * per_group):
            first = g * (dst.shape[0] // groups) + p * size
            yield g * per_group + p // 2, p % 2, size, slice(first, first + size)

    for i in range(2):
        plain_in[i].wait()
        plain_out[i].start()
        _, src, dst, _ = weights[i]
        for g in range(groups):
            loads[i][g].wait()
            for chunk, way, size, to in pieces(src, dst, g):
                dst[to, :] = src[chunk, way, :size].astype(f32)
            stores[i][g].start()
    for i in (2, 3):
        plain_in[i].wait()
        plain_out[i].start()
    for g in range(groups):
        loads[2][g].wait()
        dense = []
        for chunk, way, size, to in pieces(wg_v, qkv_v, g):
            for columns in pairs:
                parts = unpair_columns(*(wg_v[chunk, way, :size, cols].astype(f32) for cols in columns), lane)
                for cols, value in zip(columns, parts):
                    qkv_v[to, cols] = value
            dense.append(wg_v[chunk, way, :size, local3:].astype(f32))
        stores[2][g].start()
        size = dense_v.shape[1] // groups
        dense_v[:, g * size : (g + 1) * size] = jnp.concatenate(dense, axis=0).T
    last = pltpu.make_async_copy(dense_v, dense_out, dense_sem)
    last.start()
    for c in plain_out + stores[0] + stores[1] + stores[2] + [last]:
        c.wait()


def run_finish(local3, hidden, out_p, out_c, grad_p, grad_c, w1s, w2s, wg, total):
    width = out_p.shape[1]
    local = local3 // 3
    groups = 4
    shape = jax.ShapeDtypeStruct
    hbm = pl.BlockSpec(memory_space=pl.ANY)
    vmem = pl.BlockSpec(memory_space=pltpu.VMEM)
    sem = pltpu.SemaphoreType.DMA
    moved = (out_p, out_c, grad_p, grad_c)
    return pl.pallas_call(
        functools.partial(finish_kernel, groups),
        out_shape=tuple(shape(a.shape, bf16) for a in moved)
        + (shape((width,), f32),) * 4
        + (
            shape((width, local3), f32), shape((local3,), f32),
            shape((local, width), f32), shape((width,), f32),
            shape((width, hidden), f32), shape((hidden,), f32),
            shape((hidden, width), f32), shape((width,), f32),
        ),
        in_specs=[hbm] * 7 + [vmem],
        out_specs=(hbm,) * 4 + (vmem,) * 4 + (hbm, vmem) * 4,
        scratch_shapes=[pltpu.VMEM(a.shape, bf16) for a in moved + (w1s, w2s, wg)]
        + [
            pltpu.VMEM((width, local3), f32),
            pltpu.VMEM((local, width), f32),
            pltpu.VMEM((width, hidden), f32),
            pltpu.VMEM((hidden, width), f32),
            sem((4,)),
            sem((4,)),
            sem((3, groups)),
            sem((3, groups)),
            sem,
        ],
        compiler_params=pltpu.CompilerParams(vmem_limit_bytes=60 * 2**20),
        name="finish",
    )(out_p, out_c, grad_p, grad_c, w1s, w2s, wg, total)


def per_device(
    n_dp, n_tensor,
    prompt_in, cont_in, prompt_cot, cont_cot, group_of, offsets, ln1_gain, ln1_bias, ln2_gain, ln2_bias,
    qkv_weight, qkv_bias, dense_weight, dense_bias, fc1_weight, fc1_bias, fc2_weight, fc2_bias,
):
    width = prompt_in.shape[1]
    hidden = fc1_weight.shape[1]
    local3 = qkv_weight.shape[1]

    out_p, out_c, grad_p, grad_c, w1g, w2g, wg, _, total = run_layer(
        n_dp, n_tensor, min(n_dp - 1, 1), group_of, offsets, prompt_in, cont_in, prompt_cot, cont_cot,
        fc1_weight, fc2_weight, qkv_weight, dense_weight,
        ln2_gain, ln2_bias, fc1_bias, ln1_gain, ln1_bias, qkv_bias, dense_bias, fc2_bias,
    )
    return run_finish(local3, hidden, out_p, out_c, grad_p, grad_c, w1g, w2g, wg, total)


def solution(mesh):
    rows, whole, columns, segment, depth = P("dp", None), P(), P(None, "tensor"), P("tensor"), P("tensor", None)
    return jax.shard_map(
        functools.partial(per_device, mesh.shape["dp"], mesh.shape["tensor"]),
        mesh=mesh,
        in_specs=(
            rows, rows, rows, rows, whole, whole, whole, whole, whole, whole,
            columns, segment, depth, whole, columns, segment, depth, whole,
        ),
        out_specs=(
            rows, rows, rows, rows, whole, whole, whole, whole,
            columns, segment, depth, whole, columns, segment, depth, whole,
        ),
        check_vma=False,
    )
```

profile of v0, /device:TPU:0, one launch (start us, length us, event | category | flops | bytes accessed | tf_op | source)
XLA Modules:
  0.0 196.1 jit_solution(7378163388061305130)
XLA Ops:
  0.7 184.2 %layer.1 = (bf16[1024,1024]{1,0:T(8,128)(2,1)}, bf16[256,1024]{1,0:T(8,128)(2,1)}, bf16[1024,1024]{1,0:T(8,128)(2,1)}, bf16[256,1024]{1,0:T(8,128)(2,1)}, bf16[8...) custom-call(s32[16]{0:T(128)} %group_ref.1, ...), custom_call_target="tpu_custom_call" | custom-call | flops 33999998976 | bytes 40000000 | tf_op jit(solution)/shard_map/layer/pallas_call | solution.py:966
  184.9 11.0 %finish.1 = (bf16[1024,1024]{1,0:T(8,128)(2,1)}, bf16[256,1024]{1,0:T(8,128)(2,1)}, bf16[1024,1024]{1,0:T(8,128)(2,1)}, bf16[256,1024]{1,0:T(8,128)(2,1)}, f32[1...) custom-call(bf16[1024,1024]{1,0:T(8,128)(2,1)} %get-tuple-element.24, ...), custom_call_target="tpu_custom_call" | custom-call | tf_op jit(solution)/shard_map/finish/pallas_call | solution.py:1139
where the time goes:
time: 196 us
  Pallas kernels  195 us (99%)
    pallas_call x1, Pallas kernels, run_layer(): pl.pallas_call(functools.partial(layer_kernel, n_dp, n_tensor, early), ou...  184 us
    pallas_call x1, Pallas kernels, run_finish(): pl.pallas_call(functools.partial(finish_kernel, groups), out_shape=tuple(...  11 us

commit v1 on v0

--- a/solution.py
+++ b/solution.py
@@ -153,29 +153,26 @@
         self.buffer, self.arrived, self.send, self.recv, self.n = buffer, arrived, send, recv, n
         self.spot, self.after, self.before = ring_neighbours(n)
 
-    def copies(self, k):
+    def copy(self, k, way):
         n = self.n
-        ahead = lax.rem(self.spot + (2 * n - 1) - k, jnp.int32(n))
-        back = lax.rem(self.spot + 1 + k, jnp.int32(n))
-        return [
-            remote(
-                self.buffer.at[chunk, way], self.arrived.at[k, way], self.send.at[way, k], self.recv.at[way, k],
-                {"dp": device},
-            )
-            for way, (chunk, device) in enumerate(((ahead, self.after), (back, self.before)))
-        ]
-
-    def start(self, k):
-        for c in self.copies(k):
-            c.start()
-
-    def finish(self, k):
+        chunk, device = (
+            (lax.rem(self.spot + (2 * n - 1) - k, jnp.int32(n)), self.after),
+            (lax.rem(self.spot + 1 + k, jnp.int32(n)), self.before),
+        )[way]
+        return remote(
+            self.buffer.at[chunk, way], self.arrived.at[k, way], self.send.at[way, k], self.recv.at[way, k],
+            {"dp": device},
+        )
+
+    def start(self, k, ways=(0, 1)):
+        for way in ways:
+            self.copy(k, way).start()
+
+    def finish(self, k, ways=(0, 1)):
         n = self.n
-        for c in self.copies(k):
-            c.wait()
-        for way, chunk in enumerate(
-            (lax.rem(self.spot + (2 * n - 2) - k, jnp.int32(n)), lax.rem(self.spot + 2 + k, jnp.int32(n)))
-        ):
+        for way in ways:
+            self.copy(k, way).wait()
+            chunk = lax.rem(self.spot + ((2 * n - 2) - k, 2 + k)[way], jnp.int32(n))
             self.buffer[chunk, way] += self.arrived[k, way]
 
 
@@ -184,49 +181,47 @@
         self.buffer, self.send, self.recv, self.n, self.part = buffer, send, recv, n, part
         self.spot, self.after, self.before = ring_neighbours(n)
 
-    def copies(self, k):
+    def copy(self, k, way):
         n = self.n
-        ahead = lax.rem(self.spot + n - k, jnp.int32(n))
-        back = lax.rem(self.spot + k, jnp.int32(n))
-        return [
-            remote(
-                self.buffer.at[(chunk, way) + self.part], self.buffer.at[(chunk, way) + self.part],
-                self.send.at[way, k], self.recv.at[way, k], {"dp": device},
-            )
-            for way, (chunk, device) in enumerate(((ahead, self.after), (back, self.before)))
-        ]
-
-    def start(self, k):
-        for c in self.copies(k):
-            c.start()
-
-    def finish(self, k):
-        for c in self.copies(k):
-            c.wait()
+        chunk, device = (
+            (lax.rem(self.spot + n - k, jnp.int32(n)), self.after),
+            (lax.rem(self.spot + k, jnp.int32(n)), self.before),
+        )[way]
+        place = self.buffer.at[(chunk, way) + self.part]
+        return remote(place, place, self.send.at[way, k], self.recv.at[way, k], {"dp": device})
+
+    def start(self, k, ways=(0, 1)):
+        for way in ways:
+            self.copy(k, way).start()
+
+    def finish(self, k, ways=(0, 1)):
+        for way in ways:
+            self.copy(k, way).wait()
 
 
 def advance(summing, gathering, t, stop):
     n = summing.n
-
-    @pl.when(t < n - 1)
-    def _():
-        summing.finish(t)
-
-    @pl.when(t < n - 2)
-    def _():
-        summing.start(t + 1)
-
-    @pl.when((t == n - 2) & (stop > n - 1))
-    def _():
-        gathering.start(jnp.int32(0))
-
-    @pl.when((t >= n - 1) & (t < stop))
-    def _():
-        gathering.finish(t - (n - 1))
-
-    @pl.when((t >= n - 1) & (t < stop - 1))
-    def _():
-        gathering.start(t - (n - 2))
+    for way in ((0,), (1,)):
+
+        @pl.when(t < n - 1)
+        def _():
+            summing.finish(t, way)
+
+        @pl.when(t < n - 2)
+        def _():
+            summing.start(t + 1, way)
+
+        @pl.when((t == n - 2) & (stop > n - 1))
+        def _():
+            gathering.start(jnp.int32(0), way)
+
+        @pl.when((t >= n - 1) & (t < stop))
+        def _():
+            gathering.finish(t - (n - 1), way)
+
+        @pl.when((t >= n - 1) & (t < stop - 1))
+        def _():
+            gathering.start(t - (n - 2), way)
 
 
 def layer_kernel(
@@ -332,13 +327,15 @@
         for s, m in enumerate(moving):
             mine = lax.rem(t, jnp.int32(len(moving))) == s
 
-            @pl.when(mine)
-            def _():
-                m.finish(k)
-
-            @pl.when(mine & (k < n_dp - 2))
-            def _():
-                m.start(k + 1)
+            for way in ((0,), (1,)):
+
+                @pl.when(mine)
+                def _():
+                    m.finish(k, way)
+
+                @pl.when(mine & (k < n_dp - 2))
+                def _():
+                    m.start(k + 1, way)
 
     move_points = 2 * tiles + hidden // TILE
 

time: 196 us -> 197 us (level)
  no operation moved by 1% of the time
where the time goes in v1:
time: 197 us
  Pallas kernels  196 us (99%)
    pallas_call x1, Pallas kernels, run_layer(): pl.pallas_call(functools.partial(layer_kernel, n_dp, n_tensor, early), ou...  185 us
    pallas_call x1, Pallas kernels, run_finish(): pl.pallas_call(functools.partial(finish_kernel, groups), out_shape=tuple(...  11 us

profile of v1, /device:TPU:0, one launch (start us, length us, event | category | flops | bytes accessed | tf_op | source)
XLA Modules:
  0.0 196.6 jit_solution(2924245461095615234)
XLA Ops:
  0.7 184.7 %layer.1 = (bf16[1024,1024]{1,0:T(8,128)(2,1)}, bf16[256,1024]{1,0:T(8,128)(2,1)}, bf16[1024,1024]{1,0:T(8,128)(2,1)}, bf16[256,1024]{1,0:T(8,128)(2,1)}, bf16[8...) custom-call(s32[16]{0:T(128)} %group_ref.1, ...), custom_call_target="tpu_custom_call" | custom-call | flops 33999998976 | bytes 40000000 | tf_op jit(solution)/shard_map/layer/pallas_call | solution.py:963
  185.4 11.0 %finish.1 = (bf16[1024,1024]{1,0:T(8,128)(2,1)}, bf16[256,1024]{1,0:T(8,128)(2,1)}, bf16[1024,1024]{1,0:T(8,128)(2,1)}, bf16[256,1024]{1,0:T(8,128)(2,1)}, f32[1...) custom-call(bf16[1024,1024]{1,0:T(8,128)(2,1)} %get-tuple-element.24, ...), custom_call_target="tpu_custom_call" | custom-call | tf_op jit(solution)/shard_map/finish/pallas_call | solution.py:1136
